TPU v7x, 32 devices: a whole 2x2x4 slice. The times are simulated.
32 devices in a mesh: pool: 32 (over z, y, x, core).
Axes of the slice: x: 2, y: 2, z: 4, core: 2. Of those that a mesh axis runs over, the one named last changes fastest.
Arguments:
- queries: bfloat16 [32, 2, 3584], P('pool'), may hold values from -120 to 120
- kv_pool: bfloat16 [1024, 256, 2, 512], P('pool'), may hold values from -6 to 6
- lengths: int32 [32], P('pool'), may hold values from 1 to 8190, 131072 in all
- block_table: int32 [1024], P('pool'), may hold values from 0 to 1023, as said below
Outputs:
- attended: bfloat16 [32, 2, 3584], P('pool')
Inputs may be any that keep to these rules, and one draw needn't show every extreme that they name: `block_table`: a permutation of the pool blocks; with the requests numbered in groups of 1 per owner index o and G groups, the entry at place j of the 32 entries of group o is a block numbered from ((o + s_j) mod G) * 32 to that + 31, where s_j = (j * G) // 32, except s_0 = 1 when G > 32. The pool holds positions 0 to lengths + 1 of each request.
All inputs are finite; a program needn't handle non-finite values. No bound on the sum of `lengths` on one device may be relied on, other than what follows from the above.
Results may differ from a plain program's by a relative error of at most 0.0095.
Values may be sent and summed in bfloat16 or wider, within the bound.
A program may use at most 192 MiB of HBM per device.

v0:
```python
import jax
import jax.numpy as jnp
from jax import lax
from jax.sharding import PartitionSpec as P

KVH = 4
GROUP = 7
HEAD = 128
BLOCK = 256


def body(queries, kv_pool, lengths, block_table):
    every_query, every_length, every_entry = (
        lax.all_gather(queries, "pool", axis=0, tiled=True),
        lax.all_gather(lengths, "pool", axis=0, tiled=True),
        lax.all_gather(block_table, "pool", axis=0, tiled=True),
    )
    slot_count = kv_pool.shape[0]
    request_count = every_query.shape[0]
    table_width = every_entry.shape[0] // request_count
    score_scale = 1.0 / HEAD**0.5
    slot_ids = lax.axis_index("pool") * slot_count + jnp.arange(slot_count, dtype=jnp.int32)
    matches = every_entry[None, :] == slot_ids[:, None]
    entry_index = jnp.sum(
        jnp.where(matches, jnp.arange(every_entry.shape[0], dtype=jnp.int32)[None, :], 0), axis=1
    )
    owner_row = entry_index // table_width
    block_pos = entry_index % table_width
    held_query = every_query[owner_row].reshape(slot_count, 2, KVH, GROUP, HEAD)
    slot_keys = kv_pool[:, :, 0, :].reshape(slot_count, BLOCK, KVH, HEAD)
    slot_values = kv_pool[:, :, 1, :].reshape(slot_count, BLOCK, KVH, HEAD)
    scores = (
        jnp.einsum("stkgd,spkd->stkgp", held_query, slot_keys, preferred_element_type=jnp.float32)
        * score_scale
    )
    positions = block_pos[:, None] * BLOCK + jnp.arange(BLOCK, dtype=jnp.int32)[None, :]
    visible_end = every_length[owner_row][:, None] + 1 + jnp.arange(2, dtype=jnp.int32)[None, :]
    visible = positions[:, None, :] < visible_end[:, :, None]
    scores = jnp.where(visible[:, :, None, None, :], scores, -jnp.inf)
    slot_max = jnp.max(scores, axis=-1)
    member = owner_row[None, :] == jnp.arange(request_count, dtype=jnp.int32)[:, None]
    request_max = jnp.max(
        jnp.where(member[:, :, None, None, None], slot_max[None], -jnp.inf), axis=1
    )
    member_weight = member.astype(jnp.float32)
    row_peak = lax.pmax(request_max, "pool")
    unscaled = jnp.exp(scores - row_peak[owner_row][..., None])
    denominator = jnp.sum(unscaled, axis=-1)
    weights = unscaled.astype(jnp.bfloat16)
    numerator = jnp.einsum(
        "stkgp,spkd->stkgd", weights, slot_values, preferred_element_type=jnp.float32
    )
    numerator, denominator = (numerator, denominator)
    request_numer = jnp.einsum(
        "rs,stkgd->rtkgd", member_weight, numerator, precision=lax.Precision.HIGHEST
    )
    request_total = jnp.einsum(
        "rs,stkg->rtkg", member_weight, denominator, precision=lax.Precision.HIGHEST
    )
    request_numer, request_total = (request_numer, request_total)
    own_numer, own_total = (
        lax.psum_scatter(request_numer, "pool", scatter_dimension=0, tiled=True),
        lax.psum_scatter(request_total, "pool", scatter_dimension=0, tiled=True),
    )
    attended = own_numer / own_total[..., None]
    return attended.reshape(own_numer.shape[0], 2, KVH * GROUP * HEAD).astype(jnp.bfloat16)


def solution(mesh):
    placed = (P("pool", None, None), P("pool", None, None, None), P("pool"), P("pool"))
    return jax.shard_map(
        body, mesh=mesh, in_specs=placed, out_specs=P("pool", None, None), check_vma=False
    )
```

profile of v0, /device:TPU:0, one launch (start us, length us, event | category | flops | bytes accessed | tf_op | source)
XLA Modules:
  0.0 389.7 jit_solution(17582208818146803232)
XLA Ops:
  6.5 0.0 all-reduce.7.cloned.1.call-start
  7.2 0.1 dynamic-update-slice.1
  7.3 0.8 dynamic-update-slice
  8.2 42.0 %all-reduce.4 = (s32[1024]{0:T(1024)S(1)}, s32[32]{0:T(128)S(1)}) all-reduce(s32[1024]{0:T(1024)S(1)} %dynamic-update-slice, s32[32]{0:T(128)S(1)} %dynamic-update-slice.1), channel_id=1, replica_groups=mesh['pool'=32] {'pool'}, use_global_device_ids=true, to_apply=%add | all-reduce | flops 1056 | bytes 8448
  50.2 0.2 select_reduce_fusion.1
  50.4 32.8 %fusion.23 = (bf16[32,256,1,512]{3,2,1,0:T(2,128)(2,1)}, bf16[32,256,1,512]{3,2,1,0:T(2,128)(2,1)}) fusion(bf16[32,256,2,512]{3,2,1,0:T(2,128)(2,1)} %param.5), kind=kLoop, calls=%fused_computation.51 | loop fusion | bytes 33554432 | tf_op jit(solution)/shard_map/slice | solution.py:30
  83.2 35.4 %copy.52 = bf16[32,256,1,512]{1,3,0,2:T(8,128)(2,1)} copy(bf16[32,256,1,512]{3,2,1,0:T(2,128)(2,1)} %get-tuple-element.8) | data formatting | bytes 16777216
  118.7 0.7 gather_fusion
  119.4 0.1 iota_add_fusion.1
  119.5 0.1 iota_add_fusion
  119.5 0.0 copy-start
  119.5 35.4 %copy.51 = bf16[32,256,1,512]{1,3,0,2:T(8,128)(2,1)} copy(bf16[32,256,1,512]{3,2,1,0:T(2,128)(2,1)} %get-tuple-element.7) | data formatting | bytes 16777216
  155.0 0.0 copy-done
  155.0 41.5 %all_gather.11 = bf16[32,2,3584]{2,1,0:T(2,128)(2,1)S(1)} all-gather(bf16[1,2,3584]{2,1,0:T(2,128)(2,1)S(1)} %copy-done), channel_id=1, replica_groups=mesh['pool'=32] {'pool'}, dimensions={0}, use_global_device_ids=true | all-gather | bytes 473088 | tf_op jit(solution)/shard_map/all_gather | solution.py:14
  196.4 1.5 gather_fusion.1
  197.9 0.4 reshape.211
  198.3 0.1 broadcast_compare_fusion
  198.4 4.9 %bitcast_reduce_fusion = (f32[32,2,4,7]{3,1,2,0:T(2,128)S(1)}, f32[32,4,2,7,256]{4,3,2,1,0:T(8,128)S(1)}) fusion(pred[32,2,256]{2,1,0:T(4,128)(4,1)S(1)} %broadcast_compare_fusion, bf16[32,256,4,128,1]{1,3,4,2,0:T(8,128)(2,1)} %bitcast.48, bf16[32,2,4,7,128]{4,3,2,1,0:T(8,128)(2,1)S(1)} %reshape.211), kind=kOutput, calls=%fused_computation.4 | convolution fusion | flops 118814976 | bytes 10705920 | tf_op jit(solution)/shard_map/stkgd,spkd->stkgp/dot_general | solution.py:33
  203.3 0.1 copy.30
  203.5 0.3 select_reduce_fusion
  203.8 0.1 copy.31
  204.0 38.1 %pmax.7 = f32[32,2,4,7]{3,2,1,0:T(4,128)S(1)} all-reduce(f32[32,2,4,7]{3,2,1,0:T(4,128)S(1)} %copy.31), channel_id=1, replica_groups=mesh['pool'=32] {'pool'}, use_global_device_ids=true, to_apply=%region_3.4 | all-reduce | flops 1792 | bytes 14336 | tf_op jit(solution)/shard_map/pmax | solution.py:46
  242.1 0.6 gather_fusion.2
  242.7 0.1 copy.32
  242.8 5.7 %convolution_bitcast_fusion = f32[32,2,4,7,128]{4,3,1,2,0:T(8,128)S(1)} fusion(bf16[32,256,4,128,1]{1,3,4,2,0:T(8,128)(2,1)} %bitcast.49, f32[32,4,2,7,256]{4,3,2,1,0:T(8,128)S(1)} %get-tuple-element.12, f32[32,2,4,7]{3,1,2,0:T(2,128)S(1)} %copy.32, pred[32,2,256]{2,1,0:T(4,128)(4,1)S(1)} %broadcast_compare_fusion), kind=kOutput, calls=%fused_computation.9 | convolution fusion | flops 119275520 | bytes 11164672 | tf_op jit(solution)/shard_map/stkgp,spkd->stkgd/dot_general | solution.py:50
  248.5 1.1 fusion.8
  249.7 1.6 copy.36
  251.2 0.0 all-reduce.7.cloned.1.call-update
  251.2 1.2 fusion.1
  252.4 0.2 fusion.12
  252.6 0.1 copy.38
  252.7 42.3 %all-reduce.3 = f32[32,2,4,7]{3,2,1,0:T(4,128)S(1)} all-reduce(f32[32,2,4,7]{3,2,1,0:T(4,128)S(1)} %copy.38), channel_id=3, replica_groups=mesh['pool'=32] {'pool'}, use_global_device_ids=true, to_apply=%region_6.7.clone | all-reduce | flops 1792 | bytes 14336
  295.1 0.1 copy.39
  295.2 86.2 %all-reduce.7.cloned.1.call-done = f32[32,2,4,7,128]{4,2,3,1,0:T(4,128)} async-done(((f32[32,2,4,7,128]{4,2,3,1,0:T(4,128)}), f32[32,2,4,7,128]{4,2,3,1,0:T(4,128)}) %all-reduce.7.cloned.1.call-update) | async-done | bytes 917520
  381.4 0.8 fusion.14
  382.2 0.6 convert_element_type.20
  (10 shorter events, 0.1 us)
Async XLA Ops:
  6.5 374.8 %all-reduce.7.cloned.1.call-start = ((), (), s32[]{:S(2)}) async-start(), calls=%async_computation | async-start | bytes 1835008
  119.5 35.4 %copy-start = (bf16[1,2,3584]{2,1,0:T(2,128)(2,1)S(1)}, bf16[1,2,3584]{2,1,0:T(2,128)(2,1)}, u32[]{:S(2)}) copy-start(bf16[1,2,3584]{2,1,0:T(2,128)(2,1)} %param.4) | copy-start | bytes 43012
Sparse Core Ops, SparseCore 0:
  251.4 129.9 all-reduce.6
where the time goes:
time: 392 us; the launch traced here: 390 us
  blocking collectives  164 us (42%)
  local copies, waits for them, and re-layouts  110 us (28%)
  waiting for transfers between devices  86.2 us (22%)
  between operations  14.2 us (4%)
  matrix products  12 us (3%)
    unnamed x2, waiting for transfers between devices  86.2 us
    unnamed x2, blocking collectives  84.4 us
    unnamed x7, local copies, waits for them, and re-layouts  71.8 us
    all_gather x1, blocking collectives, body(): lax.all_gather(queries, 'pool', axis=0, tiled=True)  41.5 us
    pmax x1, blocking collectives, body(): row_peak = lax.pmax(request_max, 'pool')  38.1 us
    slice x1, local copies, waits for them, and re-layouts, body(): slot_keys = kv_pool[:, :, 0, :].reshape(slot_count, BLOCK, KVH, HEAD)  32.8 us
  transfers between devices with their start and end apart: 1, of which 1 were waited for; matrix products, arithmetic and copies ran while one was open for 0% of the time, Pallas kernels for 0%

commit v1 on v0

v1 whole, which is shorter than its diff:
```python
import functools

import jax
import jax.numpy as jnp
from jax import lax
from jax.experimental import pallas as pl
from jax.experimental.pallas import tpu as pltpu
from jax.sharding import PartitionSpec as P

KVH = 4
GROUP = 7
HEAD = 128
BLOCK = 256
ROWS = 16 * KVH
PLANE = 4
CORES = 2
M_ROW, L_ROW, L_LOW_ROW = 14, 15, 30
MASKED = -1e30
FLOOR = -1e20
SCALE = 1.0 / HEAD**0.5
MESH = pl.DeviceIdType.MESH


def kernel(
    n, slots, width,
    query_ref, lengths_ref, table_ref, pool_ref, out_ref,
    kv, every_query, meta, meta_scalar, spread, columns,
    core_send, core_recv, own_part, plane_send, plane_recv, plane_own, line_send, line_recv, line_own,
    kv_sem, scalar_sem,
    meta_line_s, meta_line_r, meta_plane_s, meta_plane_r, meta_core_s, meta_core_r,
    query_line_s, query_line_r, query_plane_s, query_plane_r, query_core_s, query_core_r,
    core_s, core_r, plane_s, plane_r, line_s, line_r,
):
    me = lax.axis_index("pool")
    depth = n // (PLANE * CORES)
    stride = n // width
    zz = me // (PLANE * CORES)
    pp = (me // CORES) % PLANE
    cc = me % CORES
    other = 1 - cc

    def device(z, p, c):
        return ((z * PLANE + p) * CORES + c,)

    line_to = [(zz + i) % depth for i in range(depth)]
    line_from = [(zz + depth - i) % depth for i in range(depth)]
    plane_to = [(pp + i) % PLANE for i in range(PLANE)]
    plane_from = [(pp + PLANE - i) % PLANE for i in range(PLANE)]

    chunk = slots // 4
    kv_copies = []
    for part in range(4):
        for k in range(KVH):
            copy = pltpu.make_async_copy(
                pool_ref.at[pl.ds(part * chunk, chunk), :, :, pl.ds(k * HEAD, HEAD)],
                kv.at[k, pl.ds(part * chunk, chunk)],
                kv_sem.at[part, k],
            )
            copy.start()
            kv_copies.append(copy)

    barrier = pltpu.get_barrier_semaphore()
    peers = [device(line_to[i], pp, cc) for i in range(1, depth)]
    peers += [device(zz, plane_to[i], cc) for i in range(1, PLANE)]
    peers += [device(zz, pp, other)]
    for peer in peers:
        pl.semaphore_signal(barrier, inc=1, device_id=peer, device_id_type=MESH)

    lane = lax.broadcasted_iota(jnp.int32, (1, HEAD), 1)
    own_meta = jnp.where(lane == width, lengths_ref[0], 0)
    for j in range(width):
        own_meta = jnp.where(lane == j, table_ref[j], own_meta)
    meta[cc, pp, zz] = own_meta

    spread[...] = jnp.zeros_like(spread)
    own_query = query_ref[0].astype(jnp.float32)
    for h in range(KVH * GROUP):
        row = 16 * (h // GROUP) + 2 * (h % GROUP)
        spread[row : row + 2, :] = own_query[:, h * HEAD : (h + 1) * HEAD]
    every_query[zz, cc, pp] = spread[...].astype(jnp.bfloat16)

    col = lax.broadcasted_iota(jnp.int32, (16, 2 * BLOCK), 1)
    row = lax.broadcasted_iota(jnp.int32, (16, 2 * BLOCK), 0)
    columns[...] = jnp.where(col % 2 == 0, col - 2 * (row % 2), 1 << 24)

    pl.semaphore_wait(barrier, len(peers))

    def send(src, dst, s, r, to):
        copy = pltpu.make_async_remote_copy(
            src_ref=src, dst_ref=dst, send_sem=s, recv_sem=r, device_id=to, device_id_type=MESH
        )
        return copy

    sent = []

    def go(copy):
        copy.start()
        sent.append(copy)

    def arrive(dst, s, r):
        send(dst, dst, s, r, device(zz, pp, other)).wait_recv()

    for i in range(1, depth):
        ref = meta.at[cc, pp, zz]
        go(send(ref, ref, meta_line_s.at[i - 1], meta_line_r.at[i - 1], device(line_to[i], pp, cc)))
    for i in range(1, depth):
        ref = every_query.at[zz, cc, pp]
        go(send(ref, ref, query_line_s.at[i - 1], query_line_r.at[i - 1], device(line_to[i], pp, cc)))

    def query_to_plane(i):
        ref = every_query.at[line_from[i], cc, pp]
        for d in range(1, PLANE):
            go(send(ref, ref, query_plane_s.at[i, d - 1], query_plane_r.at[i, d - 1],
                    device(zz, plane_to[d], cc)))

    query_to_plane(0)
    for i in range(1, depth):
        arrive(meta.at[cc, pp, line_from[i]], meta_line_s.at[i - 1], meta_line_r.at[i - 1])
    for d in range(1, PLANE):
        ref = meta.at[cc, pp]
        go(send(ref, ref, meta_plane_s.at[d - 1], meta_plane_r.at[d - 1], device(zz, plane_to[d], cc)))
    for i in range(1, depth):
        arrive(every_query.at[line_from[i], cc, pp], query_line_s.at[i - 1], query_line_r.at[i - 1])
        query_to_plane(i)
    for d in range(1, PLANE):
        arrive(meta.at[cc, plane_from[d]], meta_plane_s.at[d - 1], meta_plane_r.at[d - 1])
    ref = meta.at[cc]
    go(send(ref, ref, meta_core_s.at[0], meta_core_r.at[0], device(zz, pp, other)))
    order = list(range(1, depth)) + [0]
    for i in [0] + list(range(1, depth)):
        for d in range(1, PLANE):
            arrive(every_query.at[line_from[i], cc, plane_from[d]],
                   query_plane_s.at[i, d - 1], query_plane_r.at[i, d - 1])
        ref = every_query.at[line_from[i], cc]
        go(send(ref, ref, query_core_s.at[i], query_core_r.at[i], device(zz, pp, other)))
    arrive(meta.at[other], meta_core_s.at[0], meta_core_r.at[0])
    to_scalar = pltpu.make_async_copy(meta, meta_scalar, scalar_sem)
    to_scalar.start()
    to_scalar.wait()
    for copy in kv_copies:
        copy.wait()

    rows = kv.reshape(KVH, slots, 2 * BLOCK, HEAD)
    row_id = lax.broadcasted_iota(jnp.int32, (ROWS, HEAD), 0)
    lane_id = lax.broadcasted_iota(jnp.int32, (ROWS, HEAD), 1)
    eye = row_id == lane_id

    def as_column(vector):
        return jnp.sum(jnp.where(eye, vector, 0.0), axis=1, keepdims=True)

    def encode(numer, peak, total):
        high = total.astype(jnp.bfloat16).astype(jnp.float32)
        numer = jnp.where(row_id == M_ROW, peak, numer)
        numer = jnp.where(row_id == L_ROW, high, numer)
        return jnp.where(row_id == L_LOW_ROW, total - high, numer)

    def merge(states):
        states = [s.astype(jnp.float32) for s in states]
        peaks = [s[M_ROW : M_ROW + 1] for s in states]
        totals = [s[L_ROW : L_ROW + 1] + s[L_LOW_ROW : L_LOW_ROW + 1] for s in states]
        peak = functools.reduce(jnp.maximum, peaks)
        shrink = [jnp.exp(p - peak) for p in peaks]
        total = sum(a * b for a, b in zip(shrink, totals))
        numer = sum(as_column(a) * s for a, s in zip(shrink, states))
        return numer, peak, total

    def attend(z, c, p):
        request = (z * PLANE + p) * CORES + c
        away = (me + n - request) % n
        place = away if stride == 1 else jnp.where(away == 1, 0, away // stride)
        slot = lax.rem(meta_scalar[c, p, z, 0, place], slots)
        limit = 2 * (meta_scalar[c, p, z, 0, width] + 1 - place * BLOCK)
        visible = columns[...] < limit
        numers = []
        peak_row = jnp.zeros((1, HEAD), jnp.float32)
        total_row = jnp.zeros((1, HEAD), jnp.float32)
        for k in range(KVH):
            query = every_query[z, c, p, 16 * k : 16 * (k + 1), :]
            block = rows[k, slot]
            scores = lax.dot_general(
                query, block, (((1,), (1,)), ((), ())), preferred_element_type=jnp.float32
            )
            scores = jnp.where(visible, scores * SCALE, MASKED)
            peak = jnp.maximum(jnp.max(scores, axis=1, keepdims=True), FLOOR)
            peak = peak.astype(jnp.bfloat16).astype(jnp.float32)
            unscaled = jnp.exp(scores - peak)
            total = jnp.sum(unscaled, axis=1, keepdims=True)
            shifted = jnp.concatenate(
                [pltpu.roll(unscaled[:, a : a + HEAD], 1, 1) for a in range(0, 2 * BLOCK, HEAD)], axis=1
            )
            numers.append(
                jnp.dot(shifted.astype(jnp.bfloat16), block, preferred_element_type=jnp.float32)
            )
            diagonal = eye[16 * k : 16 * (k + 1)]
            peak_row += jnp.sum(jnp.where(diagonal, peak, 0.0), axis=0, keepdims=True)
            total_row += jnp.sum(jnp.where(diagonal, total, 0.0), axis=0, keepdims=True)
        return encode(jnp.concatenate(numers, axis=0), peak_row, total_row)

    def attend_into(store, z, c, p):
        if stride == 1:
            store(attend(z, c, p))
            return
        away = (me + n - ((z * PLANE + p) * CORES + c)) % n
        held = (away == 1) | ((away % stride == 0) & (away > 0))

        @pl.when(held)
        def _():
            store(attend(z, c, p))

        @pl.when(jnp.logical_not(held))
        def _():
            store(jnp.where(row_id == M_ROW, FLOOR, jnp.zeros((ROWS, HEAD), jnp.float32)))

    def compute(i):
        z = line_from[i]
        arrive(every_query.at[z, other], query_core_s.at[i], query_core_r.at[i])

        @pl.loop(0, PLANE)
        def _(p):
            def store(state):
                core_send[i, p] = state.astype(jnp.bfloat16)

            attend_into(store, z, other, p)

        go(send(core_send.at[i], core_recv.at[i], core_s.at[i], core_r.at[i], device(zz, pp, other)))

        @pl.loop(0, PLANE)
        def _(p):
            def store(state):
                own_part[i, p] = state

            attend_into(store, z, cc, p)

    def reduce_core(i):
        arrive(core_recv.at[i], core_s.at[i], core_r.at[i])
        for d in list(range(1, PLANE)) + [0]:
            p = plane_to[d]
            state = encode(*merge([own_part[i, p], core_recv[i, p]]))
            if d == 0:
                plane_own[i] = state
            else:
                plane_send[i, d - 1] = state.astype(jnp.bfloat16)
                go(send(plane_send.at[i, d - 1], plane_recv.at[i, d - 1],
                        plane_s.at[i, d - 1], plane_r.at[i, d - 1], device(zz, plane_to[d], cc)))

    def reduce_plane(i):
        for d in range(1, PLANE):
            arrive(plane_recv.at[i, d - 1], plane_s.at[i, d - 1], plane_r.at[i, d - 1])
        state = encode(*merge([plane_own[i]] + [plane_recv[i, d] for d in range(PLANE - 1)]))
        if i == 0:
            line_own[...] = state
        else:
            line_send[i - 1] = state.astype(jnp.bfloat16)
            go(send(line_send.at[i - 1], line_recv.at[i - 1], line_s.at[i - 1], line_r.at[i - 1],
                    device(line_from[i], pp, cc)))

    for step in range(depth + 2):
        if step < depth:
            compute(order[step])
        if 1 <= step <= depth:
            reduce_core(order[step - 1])
        if step >= 2:
            reduce_plane(order[step - 2])

    for i in range(1, depth):
        arrive(line_recv.at[i - 1], line_s.at[i - 1], line_r.at[i - 1])
    numer, _, total = merge([line_own[...]] + [line_recv[i] for i in range(depth - 1)])
    spread[...] = numer / as_column(total)
    for h in range(KVH * GROUP):
        row = 16 * (h // GROUP) + 2 * (h % GROUP)
        out_ref[0, :, h * HEAD : (h + 1) * HEAD] = spread[row : row + 2, :].astype(jnp.bfloat16)
    for copy in sent:
        copy.wait_send()


def body(n, queries, kv_pool, lengths, block_table):
    slots, width = kv_pool.shape[0], block_table.shape[0]
    depth = n // (PLANE * CORES)
    state, bf16, f32 = (ROWS, HEAD), jnp.bfloat16, jnp.float32
    dma = pltpu.SemaphoreType.DMA
    smem = pl.BlockSpec(memory_space=pltpu.SMEM)
    vmem = pl.BlockSpec(memory_space=pltpu.VMEM)
    return pl.pallas_call(
        functools.partial(kernel, n, slots, width),
        out_shape=jax.ShapeDtypeStruct(queries.shape, queries.dtype),
        in_specs=[vmem, smem, smem, pl.BlockSpec(memory_space=pl.ANY)],
        out_specs=vmem,
        scratch_shapes=[
            pltpu.VMEM((KVH, slots, BLOCK, 2, HEAD), bf16),
            pltpu.VMEM((depth, CORES, PLANE) + state, bf16),
            pltpu.VMEM((CORES, PLANE, depth, 1, HEAD), jnp.int32),
            pltpu.SMEM((CORES, PLANE, depth, 1, HEAD), jnp.int32),
            pltpu.VMEM(state, f32),
            pltpu.VMEM((16, 2 * BLOCK), jnp.int32),
            pltpu.VMEM((depth, PLANE) + state, bf16),
            pltpu.VMEM((depth, PLANE) + state, bf16),
            pltpu.VMEM((depth, PLANE) + state, f32),
            pltpu.VMEM((depth, PLANE - 1) + state, bf16),
            pltpu.VMEM((depth, PLANE - 1) + state, bf16),
            pltpu.VMEM((depth,) + state, f32),
            pltpu.VMEM((depth - 1,) + state, bf16),
            pltpu.VMEM((depth - 1,) + state, bf16),
            pltpu.VMEM(state, f32),
            dma((4, KVH)),
            dma,
            dma((depth - 1,)), dma((depth - 1,)), dma((PLANE - 1,)), dma((PLANE - 1,)), dma((1,)), dma((1,)),
            dma((depth - 1,)), dma((depth - 1,)), dma((depth, PLANE - 1)), dma((depth, PLANE - 1)),
            dma((depth,)), dma((depth,)),
            dma((depth,)), dma((depth,)), dma((depth, PLANE - 1)), dma((depth, PLANE - 1)),
            dma((depth - 1,)), dma((depth - 1,)),
        ],
        compiler_params=pltpu.CompilerParams(
            collective_id=0, has_side_effects=True, vmem_limit_bytes=48 * 1024 * 1024
        ),
    )(queries, lengths, block_table, kv_pool)


def solution(mesh):
    placed = (P("pool", None, None), P("pool", None, None, None), P("pool"), P("pool"))
    return jax.shard_map(
        functools.partial(body, mesh.shape["pool"]),
        mesh=mesh, in_specs=placed, out_specs=P("pool", None, None), check_vma=False,
    )
```

time: 392 us -> 71.6 us (0.18)
  blocking collectives: 164 us -> 0 us
  local copies, waits for them, and re-layouts: 110 us -> 1.96 us
  waiting for transfers between devices: 86.2 us -> 0 us
  Pallas kernels: 0 us -> 68.7 us
  between operations: 14.2 us -> 0.67 us
  matrix products: 12 us -> 0 us
    unnamed x2 -> x0, waiting for transfers between devices: 86.2 us -> none
    unnamed x2 -> x0, blocking collectives: 84.4 us -> none
    unnamed x7 -> x5, local copies, waits for them, and re-layouts: 71.8 us -> 1.96 us
    pallas_call x0 -> x1, Pallas kernels: none -> 68.7 us  [body(): pl.pallas_call(functools.partial(kernel, n, slots, width), out_shape=jax....]
    all_gather x1 -> x0, blocking collectives: 41.5 us -> none  [body(): lax.all_gather(queries, 'pool', axis=0, tiled=True)]
    pmax x1 -> x0, blocking collectives: 38.1 us -> none  [body(): row_peak = lax.pmax(request_max, 'pool')]
    slice x1 -> x0, local copies, waits for them, and re-layouts: 32.8 us -> none  [body(): slot_keys = kv_pool[:, :, 0, :].reshape(slot_count, BLOCK, KVH, HEAD)]
    dot_general x4 -> x0, matrix products: 12 us -> none  [the longest x1 5.71 us: body(): jnp.einsum('stkgp,spkd->stkgd', weights, slot_values, preferred_element_t...]
  transfers between devices with their start and end apart: 1 -> 0, of which waited for: 1 -> 0; matrix products, arithmetic and copies ran while one was open for 0% -> 0% of each run, Pallas kernels for 0% -> 0%
where the time goes in v1:
time: 71.6 us; the launch traced here: 71.4 us
  Pallas kernels  68.7 us (96%)
  local copies, waits for them, and re-layouts  1.96 us (3%)
    pallas_call x1, Pallas kernels, body(): pl.pallas_call(functools.partial(kernel, n, slots, width), out_shape=jax....  68.7 us
    unnamed x5, local copies, waits for them, and re-layouts  1.96 us

profile of v1, /device:TPU:0, one launch (start us, length us, event | category | flops | bytes accessed | tf_op | source)
XLA Modules:
  0.0 71.4 jit_solution(8112627386053456010)
XLA Ops:
  0.7 0.0 copy-start
  0.7 0.7 copy-done
  1.4 0.0 copy-start.1
  1.4 0.7 copy-done.1
  2.0 68.7 %shard_map.46 = bf16[1,2,3584]{2,1,0:T(2,128)(2,1)S(1)} custom-call(bf16[1,2,3584]{2,1,0:T(2,128)(2,1)S(1)} %copy-done, s32[1]{0:T(128)S(6)} %copy.6.lengths_ref, s32[32]{0:T(128)S(1)} %copy-done.1, bf16[32,256,2,512]{3,2,1,0:T(2,128)(2,1)} %pool_ref.1), custom_call_target="tpu_custom_call" | custom-call | tf_op jit(solution)/shard_map/pallas_call | solution.py:283
  70.8 0.6 copy.7
Async XLA Ops:
  0.7 0.7 copy-start
  1.4 0.7 copy-start.1

commit v2 on v0

v2 whole, which is shorter than its diff:
```python
import functools

import jax
import jax.numpy as jnp
from jax import lax
from jax.experimental import pallas as pl
from jax.experimental.pallas import tpu as pltpu
from jax.sharding import PartitionSpec as P

KVH = 4
GROUP = 7
HEAD = 128
BLOCK = 256
ROWS = 16 * KVH
PLANE = 4
CORES = 2
M_ROW, L_ROW, L_LOW_ROW = 14, 15, 30
MASKED = -1e30
FLOOR = -1e20
UNROLL = 4
SCALE = 1.0 / HEAD**0.5
MESH = pl.DeviceIdType.MESH


def places(n):
    me = lax.axis_index("pool")
    return me, me // (PLANE * CORES), (me // CORES) % PLANE, me % CORES


def remote(src, dst, s, r, to):
    return pltpu.make_async_remote_copy(
        src_ref=src, dst_ref=dst, send_sem=s, recv_sem=r, device_id=to, device_id_type=MESH
    )


def greet(peers):
    barrier = pltpu.get_barrier_semaphore()
    for peer in peers:
        pl.semaphore_signal(barrier, inc=1, device_id=peer, device_id_type=MESH)
    return lambda: pl.semaphore_wait(barrier, len(peers))


class Grid:
    def __init__(self, n):
        self.me, self.z, self.p, self.c = places(n)
        self.depth = n // (PLANE * CORES)
        self.other = 1 - self.c
        self.line_to = [(self.z + i) % self.depth for i in range(self.depth)]
        self.line_from = [(self.z + self.depth - i) % self.depth for i in range(self.depth)]
        self.plane_to = [(self.p + i) % PLANE for i in range(PLANE)]
        self.plane_from = [(self.p + PLANE - i) % PLANE for i in range(PLANE)]
        self.sent = []

    def at(self, z, p, c):
        return ((z * PLANE + p) * CORES + c,)

    def line(self, z):
        return self.at(z, self.p, self.c)

    def plane(self, p):
        return self.at(self.z, p, self.c)

    def core(self):
        return self.at(self.z, self.p, self.other)

    def peers(self):
        peers = [self.line(z) for z in self.line_to[1:]]
        return peers + [self.plane(p) for p in self.plane_to[1:]] + [self.core()]

    def go(self, src, dst, s, r, to):
        copy = remote(src, dst, s, r, to)
        copy.start()
        self.sent.append(copy)

    def arrive(self, dst, s, r):
        remote(dst, dst, s, r, self.core()).wait_recv()

    def finish(self):
        for copy in self.sent:
            copy.wait_send()


def gather_kernel(
    n, width,
    query_ref, lengths_ref, table_ref, every_query, meta,
    spread, length_scalar, table_scalar, small_sem,
    meta_line_s, meta_line_r, meta_plane_s, meta_plane_r, meta_core_s, meta_core_r,
    query_line_s, query_line_r, query_plane_s, query_plane_r, query_core_s, query_core_r,
):
    g = Grid(n)
    zz, pp, cc, depth = g.z, g.p, g.c, g.depth
    greeted = greet(g.peers())
    small = [
        pltpu.make_async_copy(lengths_ref, length_scalar, small_sem.at[0]),
        pltpu.make_async_copy(table_ref, table_scalar, small_sem.at[1]),
    ]
    for copy in small:
        copy.start()

    spread[...] = jnp.zeros_like(spread)
    own_query = query_ref[0].astype(jnp.float32)
    for h in range(KVH * GROUP):
        row = 16 * (h // GROUP) + 2 * (h % GROUP)
        spread[row : row + 2, :] = own_query[:, h * HEAD : (h + 1) * HEAD]
    every_query[zz, cc, pp] = spread[...].astype(jnp.bfloat16)
    for copy in small:
        copy.wait()
    lane = lax.broadcasted_iota(jnp.int32, (1, HEAD), 1)
    own_meta = jnp.where(lane == width, length_scalar[0], 0)
    for j in range(width):
        own_meta = jnp.where(lane == j, table_scalar[j], own_meta)
    meta[cc, pp, zz] = own_meta
    greeted()

    def query_to_plane(i):
        ref = every_query.at[g.line_from[i], cc, pp]
        for d in range(1, PLANE):
            g.go(ref, ref, query_plane_s.at[i, d - 1], query_plane_r.at[i, d - 1], g.plane(g.plane_to[d]))

    for i in range(1, depth):
        ref = every_query.at[zz, cc, pp]
        g.go(ref, ref, query_line_s.at[i - 1], query_line_r.at[i - 1], g.line(g.line_to[i]))
    for i in range(1, depth):
        ref = meta.at[cc, pp, zz]
        g.go(ref, ref, meta_line_s.at[i - 1], meta_line_r.at[i - 1], g.line(g.line_to[i]))
    query_to_plane(0)
    for i in range(1, depth):
        g.arrive(every_query.at[g.line_from[i], cc, pp], query_line_s.at[i - 1], query_line_r.at[i - 1])
        query_to_plane(i)
    for i in range(1, depth):
        g.arrive(meta.at[cc, pp, g.line_from[i]], meta_line_s.at[i - 1], meta_line_r.at[i - 1])
    for d in range(1, PLANE):
        ref = meta.at[cc, pp]
        g.go(ref, ref, meta_plane_s.at[d - 1], meta_plane_r.at[d - 1], g.plane(g.plane_to[d]))
    for i in range(depth):
        for d in range(1, PLANE):
            g.arrive(every_query.at[g.line_from[i], cc, g.plane_from[d]],
                     query_plane_s.at[i, d - 1], query_plane_r.at[i, d - 1])
        ref = every_query.at[g.line_from[i], cc]
        g.go(ref, ref, query_core_s.at[i], query_core_r.at[i], g.core())
    for d in range(1, PLANE):
        g.arrive(meta.at[cc, g.plane_from[d]], meta_plane_s.at[d - 1], meta_plane_r.at[d - 1])
    ref = meta.at[cc]
    g.go(ref, ref, meta_core_s.at[0], meta_core_r.at[0], g.core())
    for i in range(depth):
        g.arrive(every_query.at[g.line_from[i], g.other], query_core_s.at[i], query_core_r.at[i])
    g.arrive(meta.at[g.other], meta_core_s.at[0], meta_core_r.at[0])
    g.finish()


def state_ids():
    row_id = lax.broadcasted_iota(jnp.int32, (ROWS, HEAD), 0)
    return row_id, row_id == lax.broadcasted_iota(jnp.int32, (ROWS, HEAD), 1)


def encode(numer, peak, total):
    row_id, _ = state_ids()
    high = total.astype(jnp.bfloat16).astype(jnp.float32)
    numer = jnp.where(row_id == M_ROW, peak, numer)
    numer = jnp.where(row_id == L_ROW, high, numer)
    return jnp.where(row_id == L_LOW_ROW, total - high, numer)


def attend_kernel(
    n, slots, width,
    query_ref, meta_ref, pool_ref, out_ref,
    kv, columns, meta_scalar, held_place, count_ref, kv_sem, scalar_sem,
):
    me = lax.axis_index("pool")
    stride = n // width
    to_scalar = pltpu.make_async_copy(meta_ref, meta_scalar, scalar_sem)
    to_scalar.start()
    col = lax.broadcasted_iota(jnp.int32, (16, 2 * BLOCK), 1)
    row = lax.broadcasted_iota(jnp.int32, (16, 2 * BLOCK), 0)
    columns[...] = jnp.where(col % 2 == 0, col - 2 * (row % 2), 1 << 24)
    row_id, eye = state_ids()
    empty = jnp.where(row_id == M_ROW, FLOOR, jnp.zeros((ROWS, HEAD), jnp.float32)).astype(out_ref.dtype)
    depth = n // (PLANE * CORES)
    for z in range(depth):
        for c in range(CORES):
            for p in range(PLANE):
                out_ref[z, c, p] = empty

    def locate(place):
        step = place if stride == 1 else jnp.where(place == 0, 1, place * stride)
        request = lax.rem(me + n - step, n)
        return request // (PLANE * CORES), lax.rem(request // CORES, PLANE), lax.rem(request, CORES)

    to_scalar.wait()

    def pool_copies(index, slot):
        return [
            pltpu.make_async_copy(
                pool_ref.at[slot, :, :, pl.ds(k * HEAD, HEAD)], kv.at[k, index], kv_sem.at[k, index]
            )
            for k in range(KVH)
        ]

    count_ref[0] = 0

    @pl.loop(0, width)
    def _(place):
        z, p, c = locate(place)
        length = meta_scalar[c, p, z, 0, width]

        @pl.when(place * BLOCK < length + 2)
        def _():
            index = count_ref[0]
            held_place[index] = place
            for copy in pool_copies(index, lax.rem(meta_scalar[c, p, z, 0, place], slots)):
                copy.start()
            count_ref[0] = index + 1

    count = count_ref[0]
    rows = kv.reshape(KVH, slots, 2 * BLOCK, HEAD)

    def attend(index):
        place = held_place[index]
        z, p, c = locate(place)
        limit = 2 * (meta_scalar[c, p, z, 0, width] + 1 - place * BLOCK)
        visible = columns[...] < limit
        visible = jnp.concatenate([visible, visible], axis=0)
        numers = []
        peak_row = jnp.zeros((1, HEAD), jnp.float32)
        total_row = jnp.zeros((1, HEAD), jnp.float32)
        blank = jnp.zeros((16, HEAD), jnp.bfloat16)
        for k in range(0, KVH, 2):
            first = query_ref[z, c, p, 16 * k : 16 * (k + 1), :]
            second = query_ref[z, c, p, 16 * (k + 1) : 16 * (k + 2), :]
            query = jnp.concatenate(
                [jnp.concatenate([first, blank], axis=1), jnp.concatenate([blank, second], axis=1)], axis=0
            )
            block = jnp.concatenate([rows[k, index], rows[k + 1, index]], axis=1)
            scores = lax.dot_general(
                query, block, (((1,), (1,)), ((), ())), preferred_element_type=jnp.float32
            )
            scores = jnp.where(visible, scores * SCALE, MASKED)
            peak = jnp.maximum(jnp.max(scores, axis=1, keepdims=True), FLOOR)
            peak = peak.astype(jnp.bfloat16).astype(jnp.float32)
            unscaled = jnp.exp(scores - peak)
            total = jnp.sum(unscaled, axis=1, keepdims=True)
            shifted = jnp.concatenate(
                [pltpu.roll(unscaled[:, a : a + HEAD], 1, 1) for a in range(0, 2 * BLOCK, HEAD)], axis=1
            )
            both = jnp.dot(shifted.astype(jnp.bfloat16), block, preferred_element_type=jnp.float32)
            numers += [both[:16, :HEAD], both[16:, HEAD:]]
            diagonal = eye[16 * k : 16 * (k + 2)]
            peak_row += jnp.sum(jnp.where(diagonal, peak, 0.0), axis=0, keepdims=True)
            total_row += jnp.sum(jnp.where(diagonal, total, 0.0), axis=0, keepdims=True)
        state = encode(jnp.concatenate(numers, axis=0), peak_row, total_row)
        return (z, c, p), state.astype(out_ref.dtype)

    @pl.loop(0, (count + UNROLL - 1) // UNROLL)
    def _(step):
        for u in range(UNROLL):
            index = step * UNROLL + u

            @pl.when(index < count)
            def _():
                for copy in pool_copies(index, 0):
                    copy.wait()

        done = [attend(jnp.minimum(step * UNROLL + u, count - 1)) for u in range(UNROLL)]
        for (z, c, p), state in done:
            out_ref[z, c, p] = state


def reduce_kernel(
    n, part_ref, out_ref,
    spread, core_recv, plane_send, plane_recv, plane_own, line_send, line_recv, line_own,
    core_s, core_r, plane_s, plane_r, line_s, line_r,
):
    g = Grid(n)
    depth = g.depth
    greet(g.peers())()
    _, eye = state_ids()

    def as_column(vector):
        return jnp.sum(jnp.where(eye, vector, 0.0), axis=1, keepdims=True)

    def merge(states):
        states = [s.astype(jnp.float32) for s in states]
        peaks = [s[M_ROW : M_ROW + 1] for s in states]
        totals = [s[L_ROW : L_ROW + 1] + s[L_LOW_ROW : L_LOW_ROW + 1] for s in states]
        peak = functools.reduce(jnp.maximum, peaks)
        shrink = [jnp.exp(p - peak) for p in peaks]
        total = sum(a * b for a, b in zip(shrink, totals))
        numer = sum(as_column(a) * s for a, s in zip(shrink, states))
        return numer, peak, total

    order = list(range(1, depth)) + [0]
    for i in order:
        g.go(part_ref.at[g.line_from[i], g.other], core_recv.at[i], core_s.at[i], core_r.at[i], g.core())

    def reduce_core(i):
        g.arrive(core_recv.at[i], core_s.at[i], core_r.at[i])
        for d in list(range(1, PLANE)) + [0]:
            p = g.plane_to[d]
            state = encode(*merge([part_ref[g.line_from[i], g.c, p], core_recv[i, p]]))
            if d == 0:
                plane_own[i] = state
            else:
                plane_send[i, d - 1] = state.astype(jnp.bfloat16)
                g.go(plane_send.at[i, d - 1], plane_recv.at[i, d - 1],
                     plane_s.at[i, d - 1], plane_r.at[i, d - 1], g.plane(p))

    def reduce_plane(i):
        for d in range(1, PLANE):
            g.arrive(plane_recv.at[i, d - 1], plane_s.at[i, d - 1], plane_r.at[i, d - 1])
        state = encode(*merge([plane_own[i]] + [plane_recv[i, d] for d in range(PLANE - 1)]))
        if i == 0:
            line_own[...] = state
        else:
            line_send[i - 1] = state.astype(jnp.bfloat16)
            g.go(line_send.at[i - 1], line_recv.at[i - 1], line_s.at[i - 1], line_r.at[i - 1],
                 g.line(g.line_from[i]))

    for i in order:
        reduce_core(i)
    for i in order:
        reduce_plane(i)
    for i in range(1, depth):
        g.arrive(line_recv.at[i - 1], line_s.at[i - 1], line_r.at[i - 1])
    numer, _, total = merge([line_own[...]] + [line_recv[i] for i in range(depth - 1)])
    spread[...] = numer / as_column(total)
    for h in range(KVH * GROUP):
        row = 16 * (h // GROUP) + 2 * (h % GROUP)
        out_ref[0, :, h * HEAD : (h + 1) * HEAD] = spread[row : row + 2, :].astype(jnp.bfloat16)
    g.finish()


def body(n, queries, kv_pool, lengths, block_table):
    slots, width = kv_pool.shape[0], block_table.shape[0]
    depth = n // (PLANE * CORES)
    state, bf16, f32, i32 = (ROWS, HEAD), jnp.bfloat16, jnp.float32, jnp.int32
    dma = pltpu.SemaphoreType.DMA
    vmem, anywhere = pl.BlockSpec(memory_space=pltpu.VMEM), pl.BlockSpec(memory_space=pl.ANY)
    every = jax.ShapeDtypeStruct((depth, CORES, PLANE) + state, bf16)
    meta_shape = (CORES, PLANE, depth, 1, HEAD)

    def params(**more):
        return pltpu.CompilerParams(has_side_effects=True, vmem_limit_bytes=48 * 1024 * 1024, **more)

    every_query, meta = pl.pallas_call(
        functools.partial(gather_kernel, n, width),
        out_shape=[every, jax.ShapeDtypeStruct(meta_shape, i32)],
        in_specs=[vmem, anywhere, anywhere],
        out_specs=[vmem, vmem],
        scratch_shapes=[
            pltpu.VMEM(state, f32), pltpu.SMEM((1,), i32), pltpu.SMEM((width,), i32), dma((2,)),
            dma((depth - 1,)), dma((depth - 1,)), dma((PLANE - 1,)), dma((PLANE - 1,)), dma((1,)), dma((1,)),
            dma((depth - 1,)), dma((depth - 1,)), dma((depth, PLANE - 1)), dma((depth, PLANE - 1)),
            dma((depth,)), dma((depth,)),
        ],
        compiler_params=params(collective_id=0),
    )(queries, lengths, block_table)
    parts = pl.pallas_call(
        functools.partial(attend_kernel, n, slots, width),
        out_shape=every,
        in_specs=[vmem, anywhere, anywhere],
        out_specs=vmem,
        scratch_shapes=[
            pltpu.VMEM((KVH, slots, BLOCK, 2, HEAD), bf16),
            pltpu.VMEM((16, 2 * BLOCK), i32),
            pltpu.SMEM(meta_shape, i32),
            pltpu.SMEM((width,), i32), pltpu.SMEM((1,), i32),
            dma((KVH, slots)), dma,
        ],
        compiler_params=params(),
    )(every_query, meta, kv_pool)
    return pl.pallas_call(
        functools.partial(reduce_kernel, n),
        out_shape=jax.ShapeDtypeStruct(queries.shape, queries.dtype),
        in_specs=[vmem],
        out_specs=vmem,
        scratch_shapes=[
            pltpu.VMEM(state, f32),
            pltpu.VMEM((depth, PLANE) + state, bf16),
            pltpu.VMEM((depth, PLANE - 1) + state, bf16),
            pltpu.VMEM((depth, PLANE - 1) + state, bf16),
            pltpu.VMEM((depth,) + state, f32),
            pltpu.VMEM((depth - 1,) + state, bf16),
            pltpu.VMEM((depth - 1,) + state, bf16),
            pltpu.VMEM(state, f32),
            dma((depth,)), dma((depth,)), dma((depth, PLANE - 1)), dma((depth, PLANE - 1)),
            dma((depth - 1,)), dma((depth - 1,)),
        ],
        compiler_params=params(collective_id=1),
    )(parts)


def solution(mesh):
    placed = (P("pool", None, None), P("pool", None, None, None), P("pool"), P("pool"))
    return jax.shard_map(
        functools.partial(body, mesh.shape["pool"]),
        mesh=mesh, in_specs=placed, out_specs=P("pool", None, None), check_vma=False,
    )
```

time: 392 us -> 49.3 us (0.13)
  blocking collectives: 164 us -> 0 us
  local copies, waits for them, and re-layouts: 110 us -> 1.96 us
  waiting for transfers between devices: 86.2 us -> 0 us
  Pallas kernels: 0 us -> 46.4 us
  between operations: 14.2 us -> 0.69 us
  matrix products: 12 us -> 0 us
    unnamed x2 -> x0, waiting for transfers between devices: 86.2 us -> none
    unnamed x2 -> x0, blocking collectives: 84.4 us -> none
    unnamed x7 -> x5, local copies, waits for them, and re-layouts: 71.8 us -> 1.96 us
    pallas_call x0 -> x3, Pallas kernels: none -> 46.4 us  [the longest x1 19.8 us: body(): pl.pallas_call(functools.partial(attend_kernel, n, slots, width), out_sha...]
    all_gather x1 -> x0, blocking collectives: 41.5 us -> none  [body(): lax.all_gather(queries, 'pool', axis=0, tiled=True)]
    pmax x1 -> x0, blocking collectives: 38.1 us -> none  [body(): row_peak = lax.pmax(request_max, 'pool')]
    slice x1 -> x0, local copies, waits for them, and re-layouts: 32.8 us -> none  [body(): slot_keys = kv_pool[:, :, 0, :].reshape(slot_count, BLOCK, KVH, HEAD)]
    dot_general x4 -> x0, matrix products: 12 us -> none  [the longest x1 5.71 us: body(): jnp.einsum('stkgp,spkd->stkgd', weights, slot_values, preferred_element_t...]
  transfers between devices with their start and end apart: 1 -> 0, of which waited for: 1 -> 0; matrix products, arithmetic and copies ran while one was open for 0% -> 0% of each run, Pallas kernels for 0% -> 0%
where the time goes in v2:
time: 49.3 us; the launch traced here: 49.1 us
  Pallas kernels  46.4 us (94%)
  local copies, waits for them, and re-layouts  1.96 us (4%)
  between operations  0.69 us (1%)
    pallas_call x1, Pallas kernels, body(): pl.pallas_call(functools.partial(attend_kernel, n, slots, width), out_sha...  19.8 us
    pallas_call x1, Pallas kernels, body(): pl.pallas_call(functools.partial(gather_kernel, n, width), out_shape=[eve...  13.8 us
    pallas_call x1, Pallas kernels, body(): pl.pallas_call(functools.partial(reduce_kernel, n), out_shape=jax.ShapeDt...  12.8 us
    unnamed x5, local copies, waits for them, and re-layouts  1.96 us

profile of v2, /device:TPU:0, one launch (start us, length us, event | category | flops | bytes accessed | tf_op | source)
XLA Modules:
  0.0 49.1 jit_solution(2836628850345433059)
XLA Ops:
  0.7 0.0 copy-start
  0.7 0.7 %copy-done = bf16[1,2,3584]{2,1,0:T(2,128)(2,1)S(1)} copy-done((bf16[1,2,3584]{2,1,0:T(2,128)(2,1)S(1)}, bf16[1,2,3584]{2,1,0:T(2,128)(2,1)}, u32[]{:S(2)}) %copy-start) | copy-done | bytes 14360
  1.4 0.0 copy-start.1
  1.4 0.7 %copy-done.1 = s32[32]{0:T(128)S(1)} copy-done((s32[32]{0:T(128)S(1)}, s32[32]{0:T(128)}, u32[]{:S(2)}) %copy-start.1) | copy-done | bytes 152
  2.0 13.8 %shard_map.46 = (bf16[4,2,4,64,128]{4,3,2,1,0:T(8,128)(2,1)S(1)}, s32[2,4,4,1,128]{4,3,2,1,0:T(1,128)S(1)}) custom-call(bf16[1,2,3584]{2,1,0:T(2,128)(2,1)S(1)} %copy-done, s32[1]{0:T(128)S(6)} %copy.6.lengths_ref, s32[32]{0:T(128)S(1)} %copy-done.1), custom_call_target="tpu_custom_call" | custom-call | tf_op jit(solution)/shard_map/pallas_call | solution.py:344
  15.9 19.8 %shard_map.47.part_ref = bf16[4,2,4,64,128]{4,3,2,1,0:T(8,128)(2,1)S(1)} custom-call(bf16[4,2,4,64,128]{4,3,2,1,0:T(8,128)(2,1)S(1)} %get-tuple-element.7.query_ref, s32[2,4,4,1,128]{4,3,2,1,0:T(1,128)S(1)} %get-tuple-element.8.meta_ref, bf16[32,256,2,512]{3,2,1,0:T(2,128)(2,1)} %pool_ref.1), custom_call_target="tpu_custom_call" | custom-call | tf_op jit(solution)/shard_map/pallas_call | solution.py:357
  35.7 12.8 %shard_map.48 = bf16[1,2,3584]{2,1,0:T(2,128)(2,1)S(1)} custom-call(bf16[4,2,4,64,128]{4,3,2,1,0:T(8,128)(2,1)S(1)} %shard_map.47.part_ref), custom_call_target="tpu_custom_call" | custom-call | tf_op jit(solution)/shard_map/pallas_call | solution.py:371
  48.5 0.6 %copy.7 = bf16[1,2,3584]{2,1,0:T(2,128)(2,1)} copy(bf16[1,2,3584]{2,1,0:T(2,128)(2,1)S(1)} %shard_map.48) | data formatting | bytes 28672
Async XLA Ops:
  0.7 0.7 %copy-start = (bf16[1,2,3584]{2,1,0:T(2,128)(2,1)S(1)}, bf16[1,2,3584]{2,1,0:T(2,128)(2,1)}, u32[]{:S(2)}) copy-start(bf16[1,2,3584]{2,1,0:T(2,128)(2,1)} %query_ref.1) | copy-start | bytes 43012
  1.4 0.7 %copy-start.1 = (s32[32]{0:T(128)S(1)}, s32[32]{0:T(128)}, u32[]{:S(2)}) copy-start(s32[32]{0:T(128)} %table_ref.1) | copy-start | bytes 388
